TPU v7x, 32 devices: a whole 2x2x4 slice. The times are simulated.
32 devices in a mesh: expert: 16 (over z, y, x), token: 2 (over core).
Axes of the slice: x: 2, y: 2, z: 4, core: 2. Of those that a mesh axis runs over, the one named last changes fastest.
Arguments:
- tokens: bfloat16 [1024, 3584], P('expert', 'token'), may hold values from -6 to 6
- routes: int32 [1024, 8], P('expert'), may hold values from 0 to 15, all different within a row; in each aligned block of 64 rows (0 to 63, 64 to 127, ...) at most 64 rows name the same one
- mixing: float32 [1024, 8], P('expert'), may hold values from 0.05 to 1
- gate_weight: bfloat16 [16, 3584, 1024], P('expert', None, 'token'), may hold values from -0.09375 to 0.09375
- up_weight: bfloat16 [16, 3584, 1024], P('expert', None, 'token'), may hold values from -0.09375 to 0.09375
- down_weight: bfloat16 [16, 1024, 3584], P('expert', None, 'token'), may hold values from -0.1875 to 0.1875
Outputs:
- mixed: bfloat16 [1024, 3584], P('expert', 'token')
- hessian: float32 [16, 1024, 1024], P('expert', 'token')
Inputs may be any that keep to these rules, and one draw needn't show every extreme that they name: `routes`: each row names 8 different experts; among the 64 rows of one device no expert is named by more than 64 rows, and on some device an expert is named by exactly 64 rows; every expert is named by some row.
All inputs are finite; a program needn't handle non-finite values.
Results may differ from a plain program's by a relative error of at most 0.0058.
Values may be sent and summed in bfloat16 or wider, within the bound.
A program may use at most 128 MiB of HBM per device.

v0:
```python
import jax
import jax.numpy as jnp
from jax import lax
from jax.sharding import PartitionSpec as P


def shards(tokens, routes, mixing, gate_weight, up_weight, down_weight):
    tok_rows = tokens.shape[0]
    feat_width = tokens.shape[1]
    top_count = routes.shape[1]
    expert_count = lax.axis_size("expert")
    capacity = 2 * tok_rows * top_count // expert_count
    slot_total = expert_count * capacity
    flat_ids = routes.reshape(-1)
    chosen = (flat_ids[:, None] == jnp.arange(expert_count, dtype=jnp.int32)[None, :]).astype(
        jnp.int32
    )
    ranks = jnp.cumsum(chosen, axis=0) - chosen
    slots = jnp.sum(ranks * chosen, axis=1)
    counts = jnp.sum(chosen, axis=0)
    target = flat_ids * capacity + slots
    placing = (target[:, None] == jnp.arange(slot_total, dtype=jnp.int32)[None, :]).astype(
        jnp.bfloat16
    )
    placing = jnp.sum(placing.reshape(tok_rows, top_count, slot_total), axis=1)
    outgoing = lax.dot_general(
        placing, tokens, (((0,), (0,)), ((), ())), preferred_element_type=jnp.float32
    )
    outgoing = outgoing.astype(jnp.bfloat16).reshape(expert_count, capacity, feat_width)
    received, got_counts = (
        lax.all_to_all(outgoing, "expert", split_axis=0, concat_axis=0, tiled=True),
        lax.all_to_all(
            counts.astype(jnp.bfloat16), "expert", split_axis=0, concat_axis=0, tiled=True
        ),
    )
    rows_in = received.reshape(slot_total, feat_width)
    row_total = jnp.sum(got_counts.astype(jnp.float32))
    gate_local = gate_weight[0]
    up_local = up_weight[0]
    piece = lax.all_gather(rows_in, "token", axis=1, tiled=True)
    gate = jnp.dot(piece, gate_local, preferred_element_type=jnp.float32)
    upper = jnp.dot(piece, up_local, preferred_element_type=jnp.float32)
    hidden = (jax.nn.silu(gate) * upper).astype(jnp.bfloat16)
    down_local = down_weight[0]
    piece = lax.all_gather(hidden, "token", axis=1, tiled=True)
    out_sum = jnp.dot(piece, down_local, preferred_element_type=jnp.float32)
    outer = lax.dot_general(
        hidden, piece, (((0,), (0,)), ((), ())), preferred_element_type=jnp.float32
    )
    gram = outer
    out_sum, gram = (out_sum, gram)
    hessian = (2.0 / row_total * gram)[None]
    expert_out = out_sum.astype(jnp.bfloat16).reshape(expert_count, capacity, feat_width)
    returned = lax.all_to_all(expert_out, "expert", split_axis=0, concat_axis=0, tiled=True)
    picked = returned.reshape(slot_total, feat_width)[target]
    picked = picked.reshape(tok_rows, top_count, feat_width).astype(jnp.float32)
    mixed = jnp.sum(picked * mixing[:, :, None], axis=1).astype(jnp.bfloat16)
    return (mixed, hessian)


def solution(mesh):
    placed = (
        P("expert", "token"),
        P("expert", None),
        P("expert", None),
        P("expert", None, "token"),
        P("expert", None, "token"),
        P("expert", None, "token"),
    )
    return jax.shard_map(
        shards,
        mesh=mesh,
        in_specs=placed,
        out_specs=(P("expert", "token"), P("expert", "token", None)),
        check_vma=False,
    )
```

profile of v0, /device:TPU:8, one launch (start us, length us, event | category | flops | bytes accessed | tf_op | source)
XLA Modules:
  0.0 254.1 jit_solution(14473324830593654896)
XLA Ops:
  7.2 0.0 copy-start
  7.2 0.0 all-gather.3.cloned.1.call-start
  7.2 0.8 copy.21
  8.0 0.1 eq.43
  8.1 0.1 eq.39
  8.2 1.2 reduce-window.6
  9.4 0.2 slice_reduce_fusion
  9.7 0.2 convert_reduce_fusion
  9.8 0.1 reduce_sum.53
  9.9 0.7 fusion.9
  10.6 1.1 convolution_convert_fusion
  11.8 89.0 %all_to_all.16 = bf16[16,64,1792]{2,1,0:T(8,128)(2,1)} all-to-all(bf16[16,64,1792]{2,1,0:T(8,128)(2,1)S(1)} %bitcast.43), channel_id=1, replica_groups=mesh['expert'=16,'token'=2] {'expert'}, dimensions={0} | all-to-all | bytes 7340032 | tf_op jit(solution)/shard_map/all_to_all | solution.py:31
  100.8 0.0 all-gather.3.cloned.1.call-update
  100.8 0.0 all-gather.5.cloned.1.call-start
  100.9 17.2 %all-gather.3.cloned.1.call-done = bf16[1024,3584]{1,0:T(8,128)(2,1)} async-done(((bf16[1024,1792]{1,0:T(8,128)(2,1)}), bf16[1024,3584]{1,0:T(8,128)(2,1)}) %all-gather.3.cloned.1.call-update) | async-done | bytes 7340048 | tf_op jit(solution)/shard_map/all_gather | solution.py:40
  118.0 7.4 %fusion.2 = f32[1024,512]{1,0:T(8,128)S(1)} fusion(bf16[1024,3584]{1,0:T(8,128)(2,1)} %all-gather.3.cloned.1.call-done, bf16[1,3584,512]{2,1,0:T(8,128)(2,1)} %param.10), kind=kOutput, calls=%fused_computation.6 | convolution fusion | flops 3758096384 | bytes 13107200 | tf_op jit(solution)/shard_map/dot_general | solution.py:42
  125.5 5.2 %multiply_convert_fusion = bf16[1024,512]{1,0:T(8,128)(2,1)} fusion(f32[1024,512]{1,0:T(8,128)S(1)} %fusion.2, bf16[1024,3584]{1,0:T(8,128)(2,1)S(1)} %copy-done.4, bf16[1,3584,512]{2,1,0:T(8,128)(2,1)S(1)} %copy-done.5), kind=kOutput, calls=%fused_computation.11 | convolution fusion | flops 3761242112 | bytes 14155776 | tf_op jit(solution)/shard_map/dot_general | solution.py:41
  130.7 0.0 all-gather.5.cloned.1.call-update
  130.8 0.7 copy.26
  131.5 7.0 %all-to-all-start.2 = ((bf16[16,1,1]{2,1,0:T(2,128)(2,1)}), bf16[16,1,1]{2,1,0:T(2,128)(2,1)S(1)}, u32[]{:S(2)}, u32[]{:S(2)}) async-start(bf16[16,1,1]{2,1,0:T(2,128)(2,1)} %copy.26), calls=%async_computation.2 | async-start | bytes 16384 | tf_op jit(solution)/shard_map/all_to_all | solution.py:32
  138.4 4.2 %all-gather.5.cloned.1.call-done = bf16[1024,1024]{1,0:T(8,128)(2,1)} async-done(((bf16[1024,512]{1,0:T(8,128)(2,1)}), bf16[1024,1024]{1,0:T(8,128)(2,1)}) %all-gather.5.cloned.1.call-update) | async-done | bytes 2097168 | tf_op jit(solution)/shard_map/all_gather | solution.py:45
  142.6 8.5 %convolution_convert_fusion.1 = bf16[1024,1792]{1,0:T(8,128)(2,1)} fusion(bf16[1024,1024]{1,0:T(8,128)(2,1)} %all-gather.5.cloned.1.call-done, bf16[1,1024,1792]{2,1,0:T(8,128)(2,1)} %param.11), kind=kOutput, calls=%fused_computation.2 | convolution fusion | flops 3759931392 | bytes 9437184 | tf_op jit(solution)/shard_map/dot_general | solution.py:46
  151.1 0.0 all-to-all-done.2
  151.1 0.0 copy-start.2
  151.1 7.3 %all-to-all-start.1 = ((bf16[16,64,1792]{2,1,0:T(8,128)(2,1)}), bf16[16,64,1792]{2,1,0:T(8,128)(2,1)}, u32[]{:S(2)}, u32[]{:S(2)}) async-start(bf16[16,64,1792]{2,1,0:T(8,128)(2,1)} %bitcast.44), calls=%async_computation.1 | async-start | bytes 7340032 | tf_op jit(solution)/shard_map/all_to_all | solution.py:54
  158.4 0.1 mul.48
  158.5 0.1 copy.25
  158.6 0.6 convert_reduce_fusion.1
  159.9 2.6 %multiply_bitcast_fusion = f32[1,512,1024]{2,1,0:T(8,128)} fusion(bf16[1024,512]{1,0:T(8,128)(2,1)S(1)} %copy-done.1, bf16[1024,1024]{1,0:T(8,128)(2,1)S(1)} %copy-done.2, f32[]{:T(128)S(6)} %div.8), kind=kOutput, calls=%fused_computation.10 | convolution fusion | flops 1074266112 | bytes 5242884 | tf_op jit(solution)/shard_map/dot_general | solution.py:47
  162.5 76.0 %all-to-all-done.1 = bf16[16,64,1792]{2,1,0:T(8,128)(2,1)} async-done(((bf16[16,64,1792]{2,1,0:T(8,128)(2,1)}), bf16[16,64,1792]{2,1,0:T(8,128)(2,1)}, u32[]{:S(2)}, u32[]{:S(2)}) %all-to-all-start.1) | async-done | bytes 3670048 | tf_op jit(solution)/shard_map/all_to_all | solution.py:54
  238.5 6.5 %gather_fusion = bf16[512,1792]{1,0:T(8,128)(2,1)S(1)} fusion(bf16[1024,1792]{1,0:T(8,128)(2,1)} %bitcast.7, s32[1024]{0:T(1024)S(1)} %pad_clamp_fusion), kind=kCustom, calls=%fused_computation | custom fusion | bytes 3672064 | tf_op jit(solution)/shard_map/gather | solution.py:55
  244.9 2.3 fusion
  (17 shorter events, 0.1 us)
Async XLA Ops:
  7.2 3.5 %copy-start = (bf16[64,1792]{1,0:T(8,128)(2,1)S(1)}, bf16[64,1792]{1,0:T(8,128)(2,1)}, u32[]{:S(2)}) copy-start(bf16[64,1792]{1,0:T(8,128)(2,1)} %param.6) | copy-start | bytes 688132
  7.2 110.9 %all-gather.3.cloned.1.call-start = ((), (), s32[]{:S(2)}) async-start(), calls=%async_computation.3 | async-start | bytes 11010048 | tf_op jit(solution)/shard_map/all_gather | solution.py:40
  100.8 41.8 %all-gather.5.cloned.1.call-start = ((), (), s32[]{:S(2)}) async-start(), calls=%async_computation.4 | async-start | bytes 3145728 | tf_op jit(solution)/shard_map/all_gather | solution.py:45
  118.0 7.4 %copy-start.4 = (bf16[1024,3584]{1,0:T(8,128)(2,1)S(1)}, bf16[1024,3584]{1,0:T(8,128)(2,1)}, u32[]{:S(2)}) copy-start(bf16[1024,3584]{1,0:T(8,128)(2,1)} %all-gather.3.cloned.1.call-done) | copy-start | bytes 22020100
  118.0 7.4 %copy-start.5 = (bf16[1,3584,512]{2,1,0:T(8,128)(2,1)S(1)}, bf16[1,3584,512]{2,1,0:T(8,128)(2,1)}, u32[]{:S(2)}) copy-start(bf16[1,3584,512]{2,1,0:T(8,128)(2,1)} %param.9) | copy-start | bytes 11010052
  131.5 19.7 %all-to-all-start.2 = ((bf16[16,1,1]{2,1,0:T(2,128)(2,1)}), bf16[16,1,1]{2,1,0:T(2,128)(2,1)S(1)}, u32[]{:S(2)}, u32[]{:S(2)}) async-start(bf16[16,1,1]{2,1,0:T(2,128)(2,1)} %copy.26), calls=%async_computation.2 | async-start | bytes 16384 | tf_op jit(solution)/shard_map/all_to_all | solution.py:32
  151.1 7.4 %copy-start.3 = (f32[64,8]{0,1:T(8,128)S(1)}, f32[64,8]{0,1:T(8,128)}, u32[]{:S(2)}) copy-start(f32[64,8]{0,1:T(8,128)} %param.8) | copy-start | bytes 6148
  151.1 8.8 %copy-start.1 = (bf16[1024,512]{1,0:T(8,128)(2,1)S(1)}, bf16[1024,512]{1,0:T(8,128)(2,1)}, u32[]{:S(2)}) copy-start(bf16[1024,512]{1,0:T(8,128)(2,1)} %multiply_convert_fusion) | copy-start | bytes 3145732
  151.1 8.8 %copy-start.2 = (bf16[1024,1024]{1,0:T(8,128)(2,1)S(1)}, bf16[1024,1024]{1,0:T(8,128)(2,1)}, u32[]{:S(2)}) copy-start(bf16[1024,1024]{1,0:T(8,128)(2,1)} %all-gather.5.cloned.1.call-done) | copy-start | bytes 6291460
  151.1 87.3 %all-to-all-start.1 = ((bf16[16,64,1792]{2,1,0:T(8,128)(2,1)}), bf16[16,64,1792]{2,1,0:T(8,128)(2,1)}, u32[]{:S(2)}, u32[]{:S(2)}) async-start(bf16[16,64,1792]{2,1,0:T(8,128)(2,1)} %bitcast.44), calls=%async_computation.1 | async-start | bytes 7340032 | tf_op jit(solution)/shard_map/all_to_all | solution.py:54
Sparse Core Ops, SparseCore 0:
  100.9 17.0 all-gather.2
  130.9 11.7 all-gather.4
where the time goes:
time: 259 us; the launch traced here: 254 us
  waiting for transfers between devices  97.4 us (38%)
  blocking collectives  89 us (34%)
  matrix products  24.9 us (10%)
  between operations  14.9 us (6%)
  starting transfers between devices  14.3 us (6%)
  local copies, waits for them, and re-layouts  8.67 us (3%)
  other arithmetic  4.98 us (2%)
    all_to_all x1, blocking collectives, shards(): lax.all_to_all(outgoing, 'expert', split_axis=0, concat_axis=0, tiled=True)  89 us
    all_to_all x1, waiting for transfers between devices, shards(): lax.all_to_all(expert_out, 'expert', split_axis=0, concat_axis=0, tiled=T...  76 us
    all_gather x1, waiting for transfers between devices, shards(): piece = lax.all_gather(rows_in, 'token', axis=1, tiled=True)  17.2 us
    dot_general x1, matrix products, shards(): out_sum = jnp.dot(piece, down_local, preferred_element_type=jnp.float32)  8.46 us
    dot_general x1, matrix products, shards(): upper = jnp.dot(piece, up_local, preferred_element_type=jnp.float32)  7.42 us
    all_to_all x1, starting transfers between devices, shards(): lax.all_to_all(expert_out, 'expert', split_axis=0, concat_axis=0, tiled=T...  7.25 us
    all_to_all x1, starting transfers between devices, shards(): lax.all_to_all(counts.astype(jnp.bfloat16), 'expert', split_axis=0, conca...  6.97 us
    gather x1, local copies, waits for them, and re-layouts, shards(): picked = returned.reshape(slot_total, feat_width)[target]  6.45 us
  transfers between devices with their start and end apart: 4, of which 3 were waited for; matrix products, arithmetic and copies ran while one was open for 5% of the time, Pallas kernels for 0%

commit v1 on v0

--- a/solution.py
+++ b/solution.py
@@ -4,7 +4,7 @@
 from jax.sharding import PartitionSpec as P
 
 
-def shards(tokens, routes, mixing, gate_weight, up_weight, down_weight):
+def dispatch(tokens, routes, mixing, gate_weight, up_weight, down_weight):
     tok_rows = tokens.shape[0]
     feat_width = tokens.shape[1]
     top_count = routes.shape[1]
@@ -58,6 +58,40 @@
     return (mixed, hessian)
 
 
+def dense(tokens, routes, mixing, gate_weight, up_weight, down_weight):
+    expert_count = lax.axis_size("expert")
+    me = lax.axis_index("expert")
+    ids = jnp.arange(expert_count, dtype=jnp.int32)
+    share = jnp.sum(
+        jnp.where(routes[:, :, None] == ids[None, None, :], mixing[:, :, None], 0.0), axis=1
+    )
+    shares = lax.all_gather(share, "expert", axis=0, tiled=True)
+    mine = jnp.sum(jnp.where(ids[None, :] == me, shares, 0.0), axis=1, keepdims=True)
+    row_total = jnp.sum((mine > 0).astype(jnp.float32))
+    rows = lax.all_gather(tokens, "expert", axis=0, tiled=True)
+    rows = lax.all_gather(rows, "token", axis=1, tiled=True)
+    gate = jnp.dot(rows, gate_weight[0], preferred_element_type=jnp.float32)
+    upper = jnp.dot(rows, up_weight[0], preferred_element_type=jnp.float32)
+    hidden = jnp.where(mine > 0, jax.nn.silu(gate) * upper, 0.0).astype(jnp.bfloat16)
+    piece = lax.all_gather(hidden, "token", axis=1, tiled=True)
+    part = jnp.dot(piece, down_weight[0], preferred_element_type=jnp.float32)
+    part = (part * mine).astype(jnp.bfloat16)
+    gram = lax.dot_general(
+        hidden, piece, (((0,), (0,)), ((), ())), preferred_element_type=jnp.float32
+    )
+    hessian = (2.0 / row_total * gram)[None]
+    mixed = lax.psum_scatter(part, "expert", scatter_dimension=0, tiled=True)
+    return (mixed, hessian)
+
+
+def shards(tokens, routes, mixing, gate_weight, up_weight, down_weight):
+    tok_rows, top_count = routes.shape
+    expert_count = lax.axis_size("expert")
+    if 2 * top_count >= expert_count:
+        return dense(tokens, routes, mixing, gate_weight, up_weight, down_weight)
+    return dispatch(tokens, routes, mixing, gate_weight, up_weight, down_weight)
+
+
 def solution(mesh):
     placed = (
         P("expert", "token"),

time: 259 us -> 247 us (0.954)
  waiting for transfers between devices: 97.4 us -> 170 us
  blocking collectives: 89 us -> 32.6 us
  starting transfers between devices: 14.3 us -> 0.16 us
  local copies, waits for them, and re-layouts: 8.67 us -> 1.26 us
  other arithmetic: 4.98 us -> 0.74 us
    all_to_all x1 -> x0, blocking collectives: 89 us -> none  [shards(): lax.all_to_all(outgoing, 'expert', split_axis=0, concat_axis=0, tiled=True)]
    reduce_scatter x0 -> x1, waiting for transfers between devices: none -> 80 us  [dense(): mixed = lax.psum_scatter(part, 'expert', scatter_dimension=0, tiled=True)]
    all_to_all x2 -> x0, waiting for transfers between devices: 76 us -> none  [the longest x1 76 us: shards(): lax.all_to_all(expert_out, 'expert', split_axis=0, concat_axis=0, tiled=T...]
    all_gather x2 -> x3, waiting for transfers between devices: 21.4 us -> 89.3 us  [the longest x1 76.1 us: dense(): rows = lax.all_gather(tokens, 'expert', axis=0, tiled=True)]
    all_gather x0 -> x1, blocking collectives: none -> 32.6 us  [dense(): shares = lax.all_gather(share, 'expert', axis=0, tiled=True)]
    all_to_all x2 -> x0, starting transfers between devices: 14.2 us -> none  [the longest x1 7.25 us: shards(): lax.all_to_all(expert_out, 'expert', split_axis=0, concat_axis=0, tiled=T...]
    gather x1 -> x0, local copies, waits for them, and re-layouts: 6.45 us -> none  [shards(): picked = returned.reshape(slot_total, feat_width)[target]]
    reduce_sum x4 -> x3, other arithmetic: 3.76 us -> 0.73 us  [the longest x1 0.63 us: dense(): row_total = jnp.sum((mine > 0).astype(jnp.float32))]
  transfers between devices with their start and end apart: 4 -> 4, of which waited for: 3 -> 3; matrix products, arithmetic and copies ran while one was open for 5% -> 1% of each run, Pallas kernels for 0% -> 0%
where the time goes in v1:
time: 247 us; the launch traced here: 243 us
  waiting for transfers between devices  170 us (69%)
  blocking collectives  32.6 us (13%)
  matrix products  23.7 us (10%)
  between operations  14.6 us (6%)
    reduce_scatter x1, waiting for transfers between devices, dense(): mixed = lax.psum_scatter(part, 'expert', scatter_dimension=0, tiled=True)  80 us
    all_gather x1, waiting for transfers between devices, dense(): rows = lax.all_gather(tokens, 'expert', axis=0, tiled=True)  76.1 us
    all_gather x1, blocking collectives, dense(): shares = lax.all_gather(share, 'expert', axis=0, tiled=True)  32.6 us
    all_gather x1, waiting for transfers between devices, dense(): piece = lax.all_gather(hidden, 'token', axis=1, tiled=True)  13.1 us
    dot_general x1, matrix products, dense(): part = jnp.dot(piece, down_weight[0], preferred_element_type=jnp.float32)  8.41 us
    dot_general x1, matrix products, dense(): upper = jnp.dot(rows, up_weight[0], preferred_element_type=jnp.float32)  7.42 us
    dot_general x1, matrix products, dense(): gate = jnp.dot(rows, gate_weight[0], preferred_element_type=jnp.float32)  5.28 us
  transfers between devices with their start and end apart: 4, of which 3 were waited for; matrix products, arithmetic and copies ran while one was open for 1% of the time, Pallas kernels for 0%

profile of v1, /device:TPU:8, one launch (start us, length us, event | category | flops | bytes accessed | tf_op | source)
XLA Modules:
  0.0 243.1 jit_solution(11508411054264247745)
XLA Ops:
  7.2 0.0 copy-start.2
  7.2 0.0 copy-start.3
  7.2 0.0 all-gather.5.cloned.1.call-start
  7.2 0.7 all-gather.5.cloned.1.call-update
  7.9 0.0 all-gather.7.cloned.1.call-start
  8.0 76.1 %all-gather.5.cloned.1.call-done = bf16[1024,1792]{1,0:T(8,128)(2,1)} async-done(((bf16[64,1792]{1,0:T(8,128)(2,1)}), bf16[1024,1792]{1,0:T(8,128)(2,1)}) %all-gather.5.cloned.1.call-update) | async-done | bytes 3670032 | tf_op jit(solution)/shard_map/all_gather | solution.py:71
  84.1 0.0 all-gather.7.cloned.1.call-update
  84.1 0.0 all-gather.9.cloned.1.call-start
  84.2 0.0 copy-done.2
  84.2 0.0 copy-done.3
  84.2 32.6 %all-gather = f32[16,64,16]{1,2,0:T(8,128)S(1)} all-gather(f32[1,64,16]{1,2,0:T(8,128)S(1)} %bitcast.21), channel_id=1, replica_groups=mesh['expert'=16,'token'=2] {'expert'}, dimensions={0}, use_global_device_ids=true | all-gather | bytes 69632 | tf_op jit(solution)/shard_map/all_gather | solution.py:68
  116.9 0.1 reshape.19
  117.0 0.1 select_reduce_fusion
  117.1 0.6 convert_reduce_fusion
  117.7 0.0 all-gather.7.cloned.1.call-done
  117.7 0.0 copy-start.4
  117.7 0.0 copy-start.5
  117.7 7.4 %fusion.1 = f32[1024,512]{1,0:T(8,128)S(1)} fusion(bf16[1024,3584]{1,0:T(8,128)(2,1)} %all-gather.7.cloned.1.call-done, bf16[1,3584,512]{2,1,0:T(8,128)(2,1)} %param.10), kind=kOutput, calls=%fused_computation.2 | convolution fusion | flops 3758096384 | bytes 13107200 | tf_op jit(solution)/shard_map/dot_general | solution.py:74
  125.1 0.0 copy-done.4
  125.1 0.0 copy-done.5
  125.1 5.3 %select_convert_fusion = bf16[1024,512]{1,0:T(8,128)(2,1)} fusion(f32[1024,512]{1,0:T(8,128)S(1)} %fusion.1, bf16[1024,3584]{1,0:T(8,128)(2,1)S(1)} %copy-done.4, bf16[1,3584,512]{2,1,0:T(8,128)(2,1)S(1)} %copy-done.5, pred[1024]{0:T(1024)(128)(4,1)S(1)} %get-tuple-element.3), kind=kOutput, calls=%fused_computation.7 | convolution fusion | flops 3761766400 | bytes 14156800 | tf_op jit(solution)/shard_map/dot_general | solution.py:73
  130.4 0.0 all-gather.9.cloned.1.call-update
  130.4 0.0 reduce-scatter.2.cloned.1.call-start
  130.5 13.1 %all-gather.9.cloned.1.call-done = bf16[1024,1024]{1,0:T(8,128)(2,1)} async-done(((bf16[1024,512]{1,0:T(8,128)(2,1)}), bf16[1024,1024]{1,0:T(8,128)(2,1)}) %all-gather.9.cloned.1.call-update) | async-done | bytes 2097168 | tf_op jit(solution)/shard_map/all_gather | solution.py:76
  143.6 8.4 %multiply_convert_fusion = bf16[1024,1792]{1,0:T(8,128)(2,1)} fusion(bf16[1024,1024]{1,0:T(8,128)(2,1)} %all-gather.9.cloned.1.call-done, bf16[1,1024,1792]{2,1,0:T(8,128)(2,1)} %param.11, f32[1024]{0:T(1024)S(1)} %select_reduce_fusion), kind=kOutput, calls=%fused_computation | convolution fusion | flops 3761766400 | bytes 9441280 | tf_op jit(solution)/shard_map/dot_general | solution.py:77
  152.0 0.0 copy-start
  152.0 0.0 copy-start.1
  152.0 0.0 reduce-scatter.2.cloned.1.call-update
  152.9 0.4 copy-done
  153.3 0.7 copy-done.1
  154.0 2.6 %multiply_bitcast_fusion = f32[1,512,1024]{2,1,0:T(8,128)} fusion(bf16[1024,512]{1,0:T(8,128)(2,1)S(1)} %copy-done, bf16[1024,1024]{1,0:T(8,128)(2,1)S(1)} %copy-done.1, f32[]{:T(128)S(6)} %div.8), kind=kOutput, calls=%fused_computation.6 | convolution fusion | flops 1074266112 | bytes 5242884 | tf_op jit(solution)/shard_map/dot_general | solution.py:79
  156.5 80.0 %reduce-scatter.2.cloned.1.call-done = bf16[64,1792]{1,0:T(8,128)(2,1)} async-done(((bf16[1024,1792]{1,0:T(8,128)(2,1)}), bf16[64,1792]{1,0:T(8,128)(2,1)}) %reduce-scatter.2.cloned.1.call-update) | async-done | bytes 229392 | tf_op jit(solution)/shard_map/reduce_scatter | solution.py:83
  (3 shorter events, 0.1 us)
Async XLA Ops:
  7.2 77.0 %copy-start.2 = (f32[64,8]{0,1:T(8,128)S(1)}, f32[64,8]{0,1:T(8,128)}, u32[]{:S(2)}) copy-start(f32[64,8]{0,1:T(8,128)} %param.8) | copy-start | bytes 6148
  7.2 77.0 %copy-start.3 = (s32[64,8]{0,1:T(8,128)S(1)}, s32[64,8]{0,1:T(8,128)}, u32[]{:S(2)}) copy-start(s32[64,8]{0,1:T(8,128)} %param.7) | copy-start | bytes 6148
  7.2 76.9 %all-gather.5.cloned.1.call-start = ((), (), s32[]{:S(2)}) async-start(), calls=%async_computation.1 | async-start | bytes 3899392 | tf_op jit(solution)/shard_map/all_gather | solution.py:71
  7.9 109.8 %all-gather.7.cloned.1.call-start = ((), (), s32[]{:S(2)}) async-start(), calls=%async_computation.2 | async-start | bytes 11010048 | tf_op jit(solution)/shard_map/all_gather | solution.py:72
  84.1 59.5 %all-gather.9.cloned.1.call-start = ((), (), s32[]{:S(2)}) async-start(), calls=%async_computation.3 | async-start | bytes 3145728 | tf_op jit(solution)/shard_map/all_gather | solution.py:76
  117.7 7.4 %copy-start.4 = (bf16[1024,3584]{1,0:T(8,128)(2,1)S(1)}, bf16[1024,3584]{1,0:T(8,128)(2,1)}, u32[]{:S(2)}) copy-start(bf16[1024,3584]{1,0:T(8,128)(2,1)} %all-gather.7.cloned.1.call-done) | copy-start | bytes 22020100
  117.7 7.4 %copy-start.5 = (bf16[1,3584,512]{2,1,0:T(8,128)(2,1)S(1)}, bf16[1,3584,512]{2,1,0:T(8,128)(2,1)}, u32[]{:S(2)}) copy-start(bf16[1,3584,512]{2,1,0:T(8,128)(2,1)} %param.9) | copy-start | bytes 11010052
  130.4 106.1 %reduce-scatter.2.cloned.1.call-start = ((), (), s32[]{:S(2)}) async-start(), calls=%async_computation.4 | async-start | bytes 3899392 | tf_op jit(solution)/shard_map/reduce_scatter | solution.py:83
  152.0 1.2 copy-start
  152.0 1.9 copy-start.1
Sparse Core Ops, SparseCore 0:
  10.8 73.2 all-gather.4
  85.6 17.0 all-gather.6
  130.6 13.0 all-gather.8
  152.2 84.3 reduce-scatter.1

commit v2 on v0

--- a/solution.py
+++ b/solution.py
@@ -1,10 +1,17 @@
+import functools
+import math
+
 import jax
 import jax.numpy as jnp
 from jax import lax
+from jax.experimental import pallas as pl
+from jax.experimental.pallas import tpu as pltpu
 from jax.sharding import PartitionSpec as P
 
-
-def shards(tokens, routes, mixing, gate_weight, up_weight, down_weight):
+MESH = pl.DeviceIdType.MESH
+
+
+def dispatch(tokens, routes, mixing, gate_weight, up_weight, down_weight):
     tok_rows = tokens.shape[0]
     feat_width = tokens.shape[1]
     top_count = routes.shape[1]
@@ -58,6 +65,405 @@
     return (mixed, hessian)
 
 
+def exchange(
+    side,
+    layers,
+    tokens_hbm,
+    routes_ref,
+    mixing_ref,
+    gate_hbm,
+    up_hbm,
+    down_hbm,
+    mixed_ref,
+    hess_hbm,
+    tok,
+    table,
+    weight,
+    gate_v,
+    up_v,
+    down_v,
+    hid,
+    part,
+    in_b,
+    in_a,
+    in_z,
+    hess_v,
+    local_sem,
+    tok_send,
+    tok_recv,
+    tab_send,
+    tab_recv,
+    pair_send,
+    pair_recv,
+    hid_send,
+    hid_recv,
+    back_send,
+    back_recv,
+):
+    groups = side * side
+    rows, width = mixed_ref.shape
+    half = gate_v.shape[2]
+    me = lax.axis_index("expert")
+    core = lax.axis_index("token")
+    z, y, x = me // groups, (me // side) % side, me % side
+    stride_a = jnp.where(core == 0, side, 1)
+    stride_b = jnp.where(core == 0, 1, side)
+    pos_a = jnp.where(core == 0, y, x)
+    pos_b = jnp.where(core == 0, x, y)
+
+    def peer_z(step):
+        return me + ((z + step) % layers - z) * groups
+
+    def peer_a(step):
+        return me + ((pos_a + step) % side - pos_a) * stride_a
+
+    def peer_b(step):
+        return me + ((pos_b + step) % side - pos_b) * stride_b
+
+    def slot(dz, da, db):
+        return (da * stride_a + db * stride_b) * layers + dz
+
+    def label(dz, da, db):
+        return (da * side + db) * layers + dz
+
+    def remote(src, dst, send, recv, to, to_core=None):
+        return pltpu.make_async_remote_copy(
+            src_ref=src,
+            dst_ref=dst,
+            send_sem=send,
+            recv_sem=recv,
+            device_id=(to, core if to_core is None else to_core),
+            device_id_type=MESH,
+        )
+
+    def forward(dz, da, db):
+        if db:
+            source, to = slot(dz, da, 0), peer_b(db)
+        elif da:
+            source, to = slot(dz, 0, 0), peer_a(da)
+        else:
+            source, to = slot(0, 0, 0), peer_z(dz)
+        name = label(dz, da, db)
+        here = slot(dz, da, db)
+        return (
+            remote(table.at[source], table.at[here], tab_send.at[name], tab_recv.at[name], to),
+            remote(
+                tok.at[core, source],
+                tok.at[core, here],
+                tok_send.at[name],
+                tok_recv.at[name],
+                to,
+            ),
+        )
+
+    def start(copies):
+        for copy in copies:
+            copy.start()
+
+    def arrive(copies):
+        for copy in copies:
+            copy.wait_recv()
+
+    def across(where):
+        return remote(
+            tok.at[core, where],
+            tok.at[core, where],
+            pair_send.at[where],
+            pair_recv.at[where],
+            me,
+            1 - core,
+        )
+
+    def from_pair(where):
+        return remote(
+            tok.at[1 - core, where],
+            tok.at[1 - core, where],
+            pair_send.at[where],
+            pair_recv.at[where],
+            me,
+            1 - core,
+        )
+
+    loads = [
+        pltpu.make_async_copy(tokens_hbm, tok.at[core, 0], local_sem.at[0]),
+        pltpu.make_async_copy(gate_hbm, gate_v, local_sem.at[1]),
+        pltpu.make_async_copy(up_hbm, up_v, local_sem.at[2]),
+        pltpu.make_async_copy(down_hbm, down_v, local_sem.at[3]),
+    ]
+    start(loads)
+    barrier = pltpu.get_barrier_semaphore()
+    partners = [(peer_z(d), core) for d in range(1, layers)]
+    partners += [(peer_a(d), core) for d in range(1, side)]
+    partners += [(peer_b(d), core) for d in range(1, side)]
+    partners += [(me, 1 - core)]
+    for partner in partners:
+        pl.semaphore_signal(barrier, inc=1, device_id=partner, device_id_type=MESH)
+    named = lax.broadcasted_iota(jnp.int32, (table.shape[1], rows), 0)
+    shares = jnp.zeros((table.shape[1], rows), jnp.float32)
+    for k in range(routes_ref.shape[0]):
+        shares += jnp.where(routes_ref[k : k + 1, :] == named, mixing_ref[k : k + 1, :], 0.0)
+    table[0, :, 0:rows] = shares
+    loads[0].wait()
+    pl.semaphore_wait(barrier, len(partners))
+
+    for dz in range(1, layers):
+        start(forward(dz, 0, 0))
+    for d in range(1, side):
+        start(forward(0, d, 0))
+        start(forward(0, 0, d))
+    across(slot(0, 0, 0)).start()
+    for dz in range(1, layers):
+        arrive(forward(dz, 0, 0))
+        for d in range(1, side):
+            start(forward(dz, d, 0))
+            start(forward(dz, 0, d))
+        across(slot(dz, 0, 0)).start()
+    for da in range(1, side):
+        for dz in range(layers):
+            arrive(forward(dz, da, 0))
+            for db in range(1, side):
+                start(forward(dz, da, db))
+            across(slot(dz, da, 0)).start()
+
+    tall = layers * rows
+    tile = min(256, half)
+    diagonal = lax.broadcasted_iota(jnp.int32, (rows, rows), 0) == lax.broadcasted_iota(
+        jnp.int32, (rows, rows), 1
+    )
+
+    def up_project(g):
+        first = g * layers
+        span = pl.ds(first, layers)
+        for i in range(layers):
+            from_pair(first + i).wait_recv()
+            mine = table[first + i, pl.ds(me, 1), 0:rows]
+            column = jnp.sum(jnp.where(diagonal, mine, 0.0), axis=1, keepdims=True)
+            weight[first + i] = jnp.broadcast_to(column, weight.shape[1:])
+
+        @pl.loop(0, half // tile)
+        def _(j):
+            cols = pl.ds(pl.multiple_of(j * tile, tile), tile)
+            left = tok[0, span].reshape(tall, width)
+            right = tok[1, span].reshape(tall, width)
+            gate = jnp.dot(left, gate_v[0, :, cols], preferred_element_type=jnp.float32)
+            gate += jnp.dot(right, gate_v[1, :, cols], preferred_element_type=jnp.float32)
+            upper = jnp.dot(left, up_v[0, :, cols], preferred_element_type=jnp.float32)
+            upper += jnp.dot(right, up_v[1, :, cols], preferred_element_type=jnp.float32)
+            chosen = weight[span].reshape(tall, weight.shape[2])[:, 0:1] > 0
+            value = gate / (1.0 + jnp.exp(-gate)) * upper
+            value = jnp.where(chosen, value, 0.0).astype(jnp.bfloat16)
+            hid[core, span, :, cols] = value.reshape(layers, rows, tile)
+
+        hidden_copy(g).start()
+
+    def hidden_copy(g):
+        span = pl.ds(g * layers, layers)
+        return remote(
+            hid.at[core, span],
+            hid.at[core, span],
+            hid_send.at[g],
+            hid_recv.at[g],
+            me,
+            1 - core,
+        )
+
+    def hidden_from_pair(g):
+        span = pl.ds(g * layers, layers)
+        return remote(
+            hid.at[1 - core, span],
+            hid.at[1 - core, span],
+            hid_send.at[g],
+            hid_recv.at[g],
+            me,
+            1 - core,
+        )
+
+    def down_project(g):
+        span = pl.ds(g * layers, layers)
+        hidden_from_pair(g).wait_recv()
+
+        @pl.loop(0, width // tile)
+        def _(j):
+            cols = pl.ds(pl.multiple_of(j * tile, tile), tile)
+            left = hid[0, span].reshape(tall, half)
+            right = hid[1, span].reshape(tall, half)
+            out = jnp.dot(left, down_v[0, :, cols], preferred_element_type=jnp.float32)
+            out += jnp.dot(right, down_v[1, :, cols], preferred_element_type=jnp.float32)
+            out *= weight[span].reshape(tall, weight.shape[2])[:, 0:1]
+            part[span, :, cols] = out.astype(jnp.bfloat16).reshape(layers, rows, tile)
+
+    def back(dz, da, db):
+        name = label(dz, da, db)
+        source = part.at[slot(dz, da, db)]
+        if db:
+            target, to = in_b.at[db - 1, da * layers + dz], peer_b(side - db)
+        elif da:
+            target, to = in_a.at[da - 1, dz], peer_a(side - da)
+        else:
+            target, to = in_z.at[dz - 1], peer_z(layers - dz)
+        return remote(source, target, back_send.at[name], back_recv.at[name], to)
+
+    def summed(dz, da):
+        total = part[slot(dz, da, 0)].astype(jnp.float32)
+        for db in range(1, side):
+            back(dz, da, db).wait_recv()
+            total += in_b[db - 1, da * layers + dz].astype(jnp.float32)
+        if da == 0:
+            for d in range(1, side):
+                back(dz, d, 0).wait_recv()
+                total += in_a[d - 1, dz].astype(jnp.float32)
+        return total
+
+    for load in loads[1:]:
+        load.wait()
+    up_project(0)
+    for db in range(1, side):
+        for dz in range(layers):
+            arrive(forward(dz, 0, db))
+            across(slot(dz, 0, db)).start()
+    down_project(0)
+    edge = [g for g in range(1, groups) if g // side == 0 or g % side == 0]
+    inner = [g for g in range(1, groups) if g not in edge]
+    for g in edge:
+        up_project(g)
+    for da in range(1, side):
+        for db in range(1, side):
+            for dz in range(layers):
+                arrive(forward(dz, da, db))
+                across(slot(dz, da, db)).start()
+    for g in edge:
+        down_project(g)
+    for db in range(1, side):
+        for dz in range(layers):
+            back(dz, 0, db).start()
+    for g in inner:
+        up_project(g)
+    for g in inner:
+        down_project(g)
+    for da in range(1, side):
+        for db in range(1, side):
+            for dz in range(layers):
+                back(dz, da, db).start()
+
+    named_rows = jnp.zeros((rows, weight.shape[2]), jnp.float32)
+    for s in range(weight.shape[0]):
+        named_rows += (weight[s] > 0).astype(jnp.float32)
+    count = jnp.sum(named_rows, axis=0, keepdims=True)[:, 0:1]
+    scale = 2.0 / count
+    every = weight.shape[0] * rows
+    for h in range(2):
+
+        @pl.loop(0, half // tile)
+        def _(j):
+            cols = pl.ds(pl.multiple_of(j * tile, tile), tile)
+            gram = lax.dot_general(
+                hid[core, :, :, cols].reshape(every, tile),
+                hid[h].reshape(every, half),
+                (((0,), (0,)), ((), ())),
+                preferred_element_type=jnp.float32,
+            )
+            hess_v[cols, pl.ds(h * half, half)] = gram * scale
+
+    store = pltpu.make_async_copy(hess_v, hess_hbm, local_sem.at[0])
+    store.start()
+
+    for da in range(1, side):
+        for dz in range(layers):
+            part[slot(dz, da, 0)] = summed(dz, da).astype(jnp.bfloat16)
+            back(dz, da, 0).start()
+    for dz in range(1, layers):
+        part[dz] = summed(dz, 0).astype(jnp.bfloat16)
+        back(dz, 0, 0).start()
+    total = summed(0, 0)
+    for dz in range(1, layers):
+        back(dz, 0, 0).wait_recv()
+        total += in_z[dz - 1].astype(jnp.float32)
+    mixed_ref[...] = total.astype(jnp.bfloat16)
+
+    store.wait()
+    for da in range(side):
+        for db in range(side):
+            for dz in range(layers):
+                across(slot(dz, da, db)).wait_send()
+                if dz or da or db:
+                    for copy in forward(dz, da, db):
+                        copy.wait_send()
+                    back(dz, da, db).wait_send()
+    for g in range(groups):
+        hidden_copy(g).wait_send()
+
+
+def gathered(tokens, routes, mixing, gate_weight, up_weight, down_weight):
+    count = lax.axis_size("expert")
+    side = math.isqrt(count // 4)
+    layers = count // (side * side)
+    rows, width = tokens.shape
+    depth, half = gate_weight.shape[1:]
+    lanes = -(-rows // 128) * 128
+    bf16, f32 = jnp.bfloat16, jnp.float32
+    dma = pltpu.SemaphoreType.DMA
+    hbm = pl.BlockSpec(memory_space=pl.ANY)
+    vmem = pl.BlockSpec(memory_space=pltpu.VMEM)
+    flops = 2 * count * rows * (2 * depth * half + 2 * half * width + 2 * half * half)
+    mixed, hessian = pl.pallas_call(
+        functools.partial(exchange, side, layers),
+        out_shape=(
+            jax.ShapeDtypeStruct((rows, width), bf16),
+            jax.ShapeDtypeStruct((half, 2 * half), f32),
+        ),
+        in_specs=[hbm, vmem, vmem, hbm, hbm, hbm],
+        out_specs=(vmem, hbm),
+        scratch_shapes=[
+            pltpu.VMEM((2, count, rows, width), bf16),
+            pltpu.VMEM((count, count, lanes), f32),
+            pltpu.VMEM((count, rows, 128), f32),
+            pltpu.VMEM((2, width, half), bf16),
+            pltpu.VMEM((2, width, half), bf16),
+            pltpu.VMEM((2, half, width), bf16),
+            pltpu.VMEM((2, count, rows, half), bf16),
+            pltpu.VMEM((count, rows, width), bf16),
+            pltpu.VMEM((side - 1, side * layers, rows, width), bf16),
+            pltpu.VMEM((side - 1, layers, rows, width), bf16),
+            pltpu.VMEM((layers - 1, rows, width), bf16),
+            pltpu.VMEM((half, 2 * half), f32),
+            dma((4,)),
+            dma((count,)),
+            dma((count,)),
+            dma((count,)),
+            dma((count,)),
+            dma((count,)),
+            dma((count,)),
+            dma((side * side,)),
+            dma((side * side,)),
+            dma((count,)),
+            dma((count,)),
+        ],
+        compiler_params=pltpu.CompilerParams(
+            collective_id=0, has_side_effects=True, vmem_limit_bytes=60 * 2**20
+        ),
+        cost_estimate=pl.CostEstimate(
+            flops=flops,
+            bytes_accessed=2 * (2 * depth * half + 2 * half * width),
+            transcendentals=count * rows * half,
+        ),
+    )(
+        tokens,
+        routes.T,
+        mixing.T,
+        gate_weight.reshape(2, width, half),
+        up_weight.reshape(2, width, half),
+        down_weight.reshape(2, half, width),
+    )
+    return (mixed, hessian[None])
+
+
+def shards(tokens, routes, mixing, gate_weight, up_weight, down_weight):
+    expert_count = lax.axis_size("expert")
+    if 2 * routes.shape[1] >= expert_count:
+        return gathered(tokens, routes, mixing, gate_weight, up_weight, down_weight)
+    return dispatch(tokens, routes, mixing, gate_weight, up_weight, down_weight)
+
+
 def solution(mesh):
     placed = (
         P("expert", "token"),

time: 259 us -> 113 us (0.44)
  the two profiles are of different devices: /device:TPU:8 before, /device:TPU:0 now
where the time goes in v2:
time: 113 us
  Pallas kernels  108 us (96%)
  local copies, waits for them, and re-layouts  4.8 us (4%)
    pallas_call x1, Pallas kernels, gathered(): pl.pallas_call(functools.partial(exchange, side, layers), out_shape=(jax....  108 us
    unnamed x2, local copies, waits for them, and re-layouts  4.8 us

profile of v2, /device:TPU:0, one launch (start us, length us, event | category | flops | bytes accessed | tf_op | source)
XLA Modules:
  0.0 113.2 jit_solution(10455399356901384433)
XLA Ops:
  0.6 107.8 %shard_map.77 = (bf16[64,1792]{1,0:T(8,128)(2,1)}, f32[512,1024]{1,0:T(8,128)}) custom-call(bf16[64,1792]{1,0:T(8,128)(2,1)} %tokens_hbm.1, s32[8,64]{1,0:T(8,128)} %bitcast.10, f32[8,64]{1,0:T(8,128)} %bitcast.11, bf16[2,1792,512]{2,1,0:T(8,128)(2,1)} %bitcast.7, bf16[2,1792,512]{2,1,0:T(8,128)(2,1)} %bitcast.8, bf16[2,512,1792]{2,1,0:T(8,128)(2,1)} %bitcast.9), custom_call_target="tpu_custom_call" | custom-call | flops 12348030976 | bytes 11010048 | tf_op jit(solution)/shard_map/pallas_call | solution.py:408
  108.4 1.6 %copy.10 = bf16[64,1792]{1,0:T(8,128)(2,1)} copy(bf16[64,1792]{1,0:T(8,128)(2,1)} %get-tuple-element.8) | data formatting | bytes 458752
  110.1 3.2 %copy.11 = f32[1,512,1024]{2,1,0:T(8,128)} copy(f32[1,512,1024]{2,1,0:T(8,128)} %bitcast.6) | data formatting | bytes 4194304

commit v3 on v2

--- a/solution.py
+++ b/solution.py
@@ -99,6 +99,7 @@
     hid_recv,
     back_send,
     back_recv,
+    chain_send,
 ):
     groups = side * side
     rows, width = mixed_ref.shape
@@ -206,24 +207,79 @@
     loads[0].wait()
     pl.semaphore_wait(barrier, len(partners))
 
-    for dz in range(1, layers):
-        start(forward(dz, 0, 0))
-    for d in range(1, side):
-        start(forward(0, d, 0))
-        start(forward(0, 0, d))
-    across(slot(0, 0, 0)).start()
-    for dz in range(1, layers):
-        arrive(forward(dz, 0, 0))
+    orders = [
+        sorted(range(1, layers), key=lambda d: (d if d <= place else layers - d, d))
+        for place in range(layers)
+    ]
+
+    def coming(k):
+        return sum(jnp.where(z == place, orders[place][k], 0) for place in range(layers))
+
+    def chain(s, way, here):
+        source = slot(s, 0, 0)
+        there = slot(here, 0, 0)
+        to = me + (groups if way == 0 else -groups)
+        return (
+            remote(
+                table.at[source],
+                table.at[there],
+                chain_send.at[2 + way, s],
+                tab_recv.at[here],
+                to,
+            ),
+            remote(
+                tok.at[core, source],
+                tok.at[core, there],
+                chain_send.at[way, s],
+                tok_recv.at[here],
+                to,
+            ),
+        )
+
+    def along(s, act):
+        @pl.when((z < layers - 1) & (s <= z))
+        def _():
+            for copy in chain(s, 0, s + 1):
+                act(copy)
+
+        @pl.when((z > 0) & ((s == 0) | (s > z)))
+        def _():
+            for copy in chain(s, 1, (s + layers - 1) % layers):
+                act(copy)
+
+    def spread(dz):
+        along(dz, lambda copy: copy.start())
         for d in range(1, side):
             start(forward(dz, d, 0))
             start(forward(dz, 0, d))
         across(slot(dz, 0, 0)).start()
-    for da in range(1, side):
-        for dz in range(layers):
+
+    def turn(dz):
+        for da in range(1, side):
             arrive(forward(dz, da, 0))
             for db in range(1, side):
                 start(forward(dz, da, db))
             across(slot(dz, da, 0)).start()
+
+    def straight(dz):
+        for db in range(1, side):
+            arrive(forward(dz, 0, db))
+            across(slot(dz, 0, db)).start()
+
+    def last(dz):
+        for da in range(1, side):
+            for db in range(1, side):
+                arrive(forward(dz, da, db))
+                across(slot(dz, da, db)).start()
+
+    sequence = [0] + [coming(k) for k in range(layers - 1)]
+    spread(sequence[0])
+    for k in range(1, layers):
+        arrive(forward(sequence[k], 0, 0))
+        spread(sequence[k])
+        turn(sequence[k - 1])
+        straight(sequence[k - 1])
+    turn(sequence[-1])
 
     tall = layers * rows
     tile = min(256, half)
@@ -314,36 +370,35 @@
                 total += in_a[d - 1, dz].astype(jnp.float32)
         return total
 
+    def send_back(da, db):
+        for dz in range(layers):
+            back(dz, da, db).start()
+
     for load in loads[1:]:
         load.wait()
     up_project(0)
+    straight(sequence[-1])
+    edge = [g for g in range(1, groups) if g // side == 0 or g % side == 0]
+    for g in edge[:-1]:
+        up_project(g)
+    for k in range(layers // 2):
+        last(sequence[k])
+    up_project(edge[-1])
+    for k in range(layers // 2, layers):
+        last(sequence[k])
     for db in range(1, side):
-        for dz in range(layers):
-            arrive(forward(dz, 0, db))
-            across(slot(dz, 0, db)).start()
-    down_project(0)
-    edge = [g for g in range(1, groups) if g // side == 0 or g % side == 0]
+        down_project(db * stride_b)
+        send_back(0, db)
     inner = [g for g in range(1, groups) if g not in edge]
-    for g in edge:
+    for g in inner:
         up_project(g)
     for da in range(1, side):
-        for db in range(1, side):
-            for dz in range(layers):
-                arrive(forward(dz, da, db))
-                across(slot(dz, da, db)).start()
-    for g in edge:
-        down_project(g)
-    for db in range(1, side):
-        for dz in range(layers):
-            back(dz, 0, db).start()
-    for g in inner:
-        up_project(g)
-    for g in inner:
-        down_project(g)
+        down_project(da * stride_a)
     for da in range(1, side):
         for db in range(1, side):
-            for dz in range(layers):
-                back(dz, da, db).start()
+            down_project(da * stride_a + db * stride_b)
+            send_back(da, db)
+    down_project(0)
 
     named_rows = jnp.zeros((rows, weight.shape[2]), jnp.float32)
     for s in range(weight.shape[0]):
@@ -367,11 +422,12 @@
     store = pltpu.make_async_copy(hess_v, hess_hbm, local_sem.at[0])
     store.start()
 
+    far = sorted(range(1, layers), key=lambda d: -min(d, layers - d))
     for da in range(1, side):
-        for dz in range(layers):
+        for dz in far + [0]:
             part[slot(dz, da, 0)] = summed(dz, da).astype(jnp.bfloat16)
             back(dz, da, 0).start()
-    for dz in range(1, layers):
+    for dz in far:
         part[dz] = summed(dz, 0).astype(jnp.bfloat16)
         back(dz, 0, 0).start()
     total = summed(0, 0)
@@ -385,12 +441,27 @@
         for db in range(side):
             for dz in range(layers):
                 across(slot(dz, da, db)).wait_send()
-                if dz or da or db:
+                if da or db:
                     for copy in forward(dz, da, db):
                         copy.wait_send()
+                if dz or da or db:
                     back(dz, da, db).wait_send()
+    for dz in range(layers):
+        along(dz, lambda copy: copy.wait_send())
     for g in range(groups):
         hidden_copy(g).wait_send()
+
+
+def settle(mixed_in, hess_in, mixed_out, hess_out, sems):
+    quarter = hess_in.shape[0] // 4
+    copies = [pltpu.make_async_copy(mixed_in, mixed_out, sems.at[4])]
+    for i in range(4):
+        span = pl.ds(i * quarter, quarter)
+        copies.append(pltpu.make_async_copy(hess_in.at[span], hess_out.at[span], sems.at[i]))
+    for copy in copies:
+        copy.start()
+    for copy in copies:
+        copy.wait()
 
 
 def gathered(tokens, routes, mixing, gate_weight, up_weight, down_weight):
@@ -437,6 +508,7 @@
             dma((side * side,)),
             dma((count,)),
             dma((count,)),
+            dma((4, layers)),
         ],
         compiler_params=pltpu.CompilerParams(
             collective_id=0, has_side_effects=True, vmem_limit_bytes=60 * 2**20
@@ -454,6 +526,17 @@
         up_weight.reshape(2, width, half),
         down_weight.reshape(2, half, width),
     )
+    mixed, hessian = pl.pallas_call(
+        settle,
+        out_shape=(
+            jax.ShapeDtypeStruct(mixed.shape, bf16),
+            jax.ShapeDtypeStruct(hessian.shape, f32),
+        ),
+        in_specs=[hbm, hbm],
+        out_specs=(hbm, hbm),
+        scratch_shapes=[dma((5,))],
+        compiler_params=pltpu.CompilerParams(vmem_limit_bytes=60 * 2**20),
+    )(mixed, hessian)
     return (mixed, hessian[None])
 
 

time: 113 us -> 161 us (1.42)
  the two profiles are of different devices: /device:TPU:0 before, /device:TPU:8 now
where the time goes in v3:
time: 161 us; the launch traced here: 160 us
  Pallas kernels  160 us (99%)
    pallas_call x1, Pallas kernels, gathered(): pl.pallas_call(functools.partial(exchange, side, layers), out_shape=(jax....  88 us
    pallas_call x1, Pallas kernels, gathered(): pl.pallas_call(settle, out_shape=(jax.ShapeDtypeStruct(mixed.shape, bf16)...  71.6 us

profile of v3, /device:TPU:8, one launch (start us, length us, event | category | flops | bytes accessed | tf_op | source)
XLA Modules:
  0.0 160.3 jit_solution(14475011395234327354)
XLA Ops:
  0.6 88.0 %shard_map.77 = (bf16[64,1792]{1,0:T(8,128)(2,1)}, f32[512,1024]{1,0:T(8,128)}) custom-call(bf16[64,1792]{1,0:T(8,128)(2,1)} %tokens_hbm.1, s32[8,64]{1,0:T(8,128)} %bitcast.10, f32[8,64]{1,0:T(8,128)} %bitcast.11, bf16[2,1792,512]{2,1,0:T(8,128)(2,1)} %bitcast.6, bf16[2,1792,512]{2,1,0:T(8,128)(2,1)} %bitcast.7, bf16[2,512,1792]{2,1,0:T(8,128)(2,1)} %bitcast.8), custom_call_target="tpu_custom_call" | custom-call | flops 12348030976 | bytes 11010048 | tf_op jit(solution)/shard_map/pallas_call | solution.py:479
  88.7 71.6 %shard_map.78 = (bf16[64,1792]{1,0:T(8,128)(2,1)}, f32[512,1024]{1,0:T(8,128)}) custom-call(bf16[64,1792]{1,0:T(8,128)(2,1)} %get-tuple-element.6.mixed_in, f32[512,1024]{1,0:T(8,128)} %get-tuple-element.7.hess_in), custom_call_target="tpu_custom_call" | custom-call | tf_op jit(solution)/shard_map/pallas_call | solution.py:529

commit v4 on v3

--- a/solution.py
+++ b/solution.py
@@ -257,9 +257,12 @@
     def turn(dz):
         for da in range(1, side):
             arrive(forward(dz, da, 0))
+            across(slot(dz, da, 0)).start()
+
+    def finish(dz):
+        for da in range(1, side):
             for db in range(1, side):
                 start(forward(dz, da, db))
-            across(slot(dz, da, 0)).start()
 
     def straight(dz):
         for db in range(1, side):
@@ -279,7 +282,10 @@
         spread(sequence[k])
         turn(sequence[k - 1])
         straight(sequence[k - 1])
+    for k in range(layers - 1):
+        finish(sequence[k])
     turn(sequence[-1])
+    finish(sequence[-1])
 
     tall = layers * rows
     tile = min(256, half)
@@ -370,8 +376,10 @@
                 total += in_a[d - 1, dz].astype(jnp.float32)
         return total
 
+    far = sorted(range(1, layers), key=lambda d: -min(d, layers - d))
+
     def send_back(da, db):
-        for dz in range(layers):
+        for dz in far + [0]:
             back(dz, da, db).start()
 
     for load in loads[1:]:
@@ -406,8 +414,8 @@
     count = jnp.sum(named_rows, axis=0, keepdims=True)[:, 0:1]
     scale = 2.0 / count
     every = weight.shape[0] * rows
-    for h in range(2):
-
+
+    def hessian_half(h):
         @pl.loop(0, half // tile)
         def _(j):
             cols = pl.ds(pl.multiple_of(j * tile, tile), tile)
@@ -419,14 +427,14 @@
             )
             hess_v[cols, pl.ds(h * half, half)] = gram * scale
 
-    store = pltpu.make_async_copy(hess_v, hess_hbm, local_sem.at[0])
-    store.start()
-
-    far = sorted(range(1, layers), key=lambda d: -min(d, layers - d))
+    hessian_half(0)
     for da in range(1, side):
         for dz in far + [0]:
             part[slot(dz, da, 0)] = summed(dz, da).astype(jnp.bfloat16)
             back(dz, da, 0).start()
+    hessian_half(1)
+    store = pltpu.make_async_copy(hess_v, hess_hbm, local_sem.at[0])
+    store.start()
     for dz in far:
         part[dz] = summed(dz, 0).astype(jnp.bfloat16)
         back(dz, 0, 0).start()
@@ -452,16 +460,21 @@
         hidden_copy(g).wait_send()
 
 
-def settle(mixed_in, hess_in, mixed_out, hess_out, sems):
-    quarter = hess_in.shape[0] // 4
-    copies = [pltpu.make_async_copy(mixed_in, mixed_out, sems.at[4])]
-    for i in range(4):
-        span = pl.ds(i * quarter, quarter)
-        copies.append(pltpu.make_async_copy(hess_in.at[span], hess_out.at[span], sems.at[i]))
-    for copy in copies:
+def settle(mixed_in, hess_in, mixed_out, hess_out, mixed_v, hess_v, sems):
+    pieces = 4
+    span = hess_in.shape[0] // pieces
+    moves = [(mixed_in, mixed_v, mixed_out)]
+    for i in range(pieces):
+        moves.append([ref.at[pl.ds(i * span, span)] for ref in (hess_in, hess_v, hess_out)])
+    comes = [pltpu.make_async_copy(m[0], m[1], sems.at[0, i]) for i, m in enumerate(moves)]
+    goes = [pltpu.make_async_copy(m[1], m[2], sems.at[1, i]) for i, m in enumerate(moves)]
+    for copy in comes:
         copy.start()
-    for copy in copies:
-        copy.wait()
+    for come, go in zip(comes, goes):
+        come.wait()
+        go.start()
+    for go in goes:
+        go.wait()
 
 
 def gathered(tokens, routes, mixing, gate_weight, up_weight, down_weight):
@@ -534,7 +547,11 @@
         ),
         in_specs=[hbm, hbm],
         out_specs=(hbm, hbm),
-        scratch_shapes=[dma((5,))],
+        scratch_shapes=[
+            pltpu.VMEM(mixed.shape, bf16),
+            pltpu.VMEM(hessian.shape, f32),
+            dma((2, 5)),
+        ],
         compiler_params=pltpu.CompilerParams(vmem_limit_bytes=60 * 2**20),
     )(mixed, hessian)
     return (mixed, hessian[None])

time: 161 us -> 94.8 us (0.59)
  Pallas kernels: 160 us -> 93.4 us
    pallas_call x1, Pallas kernels: 71.6 us -> 2.56 us  [gathered(): pl.pallas_call(settle, out_shape=(jax.ShapeDtypeStruct(mixed.shape, bf16)...]
    pallas_call x1, Pallas kernels: 88 us -> 90.8 us  [gathered(): pl.pallas_call(functools.partial(exchange, side, layers), out_shape=(jax....]
where the time goes in v4:
time: 94.8 us; the launch traced here: 94 us
  Pallas kernels  93.4 us (99%)
    pallas_call x1, Pallas kernels, gathered(): pl.pallas_call(functools.partial(exchange, side, layers), out_shape=(jax....  90.8 us
    pallas_call x1, Pallas kernels, gathered(): pl.pallas_call(settle, out_shape=(jax.ShapeDtypeStruct(mixed.shape, bf16)...  2.56 us

profile of v4, /device:TPU:8, one launch (start us, length us, event | category | flops | bytes accessed | tf_op | source)
XLA Modules:
  0.0 94.0 jit_solution(1211361875278749056)
XLA Ops:
  0.6 90.8 %shard_map.77 = (bf16[64,1792]{1,0:T(8,128)(2,1)}, f32[512,1024]{1,0:T(8,128)}) custom-call(bf16[64,1792]{1,0:T(8,128)(2,1)} %tokens_hbm.1, s32[8,64]{1,0:T(8,128)} %bitcast.10, f32[8,64]{1,0:T(8,128)} %bitcast.11, bf16[2,1792,512]{2,1,0:T(8,128)(2,1)} %bitcast.6, bf16[2,1792,512]{2,1,0:T(8,128)(2,1)} %bitcast.7, bf16[2,512,1792]{2,1,0:T(8,128)(2,1)} %bitcast.8), custom_call_target="tpu_custom_call" | custom-call | flops 12348030976 | bytes 11010048 | tf_op jit(solution)/shard_map/pallas_call | solution.py:492
  91.5 2.6 %shard_map.78 = (bf16[64,1792]{1,0:T(8,128)(2,1)}, f32[512,1024]{1,0:T(8,128)}) custom-call(bf16[64,1792]{1,0:T(8,128)(2,1)} %get-tuple-element.6.mixed_in, f32[512,1024]{1,0:T(8,128)} %get-tuple-element.7.hess_in), custom_call_target="tpu_custom_call" | custom-call | tf_op jit(solution)/shard_map/pallas_call | solution.py:542

commit v5 on v4

--- a/solution.py
+++ b/solution.py
@@ -257,12 +257,9 @@
     def turn(dz):
         for da in range(1, side):
             arrive(forward(dz, da, 0))
-            across(slot(dz, da, 0)).start()
-
-    def finish(dz):
-        for da in range(1, side):
             for db in range(1, side):
                 start(forward(dz, da, db))
+            across(slot(dz, da, 0)).start()
 
     def straight(dz):
         for db in range(1, side):
@@ -282,10 +279,7 @@
         spread(sequence[k])
         turn(sequence[k - 1])
         straight(sequence[k - 1])
-    for k in range(layers - 1):
-        finish(sequence[k])
     turn(sequence[-1])
-    finish(sequence[-1])
 
     tall = layers * rows
     tile = min(256, half)
@@ -293,10 +287,16 @@
         jnp.int32, (rows, rows), 1
     )
 
-    def up_project(g):
+    def row_weights(span, count):
+        wide = weight[span].reshape(count, weight.shape[2])
+        return jnp.concatenate([wide] * (tile // weight.shape[2]), axis=1)
+
+    def up_project(g, many=1):
         first = g * layers
-        span = pl.ds(first, layers)
-        for i in range(layers):
+        blocks = many * layers
+        tall = blocks * rows
+        span = pl.ds(first, blocks)
+        for i in range(blocks):
             from_pair(first + i).wait_recv()
             mine = table[first + i, pl.ds(me, 1), 0:rows]
             column = jnp.sum(jnp.where(diagonal, mine, 0.0), axis=1, keepdims=True)
@@ -311,12 +311,13 @@
             gate += jnp.dot(right, gate_v[1, :, cols], preferred_element_type=jnp.float32)
             upper = jnp.dot(left, up_v[0, :, cols], preferred_element_type=jnp.float32)
             upper += jnp.dot(right, up_v[1, :, cols], preferred_element_type=jnp.float32)
-            chosen = weight[span].reshape(tall, weight.shape[2])[:, 0:1] > 0
+            chosen = row_weights(span, tall) > 0
             value = gate / (1.0 + jnp.exp(-gate)) * upper
             value = jnp.where(chosen, value, 0.0).astype(jnp.bfloat16)
-            hid[core, span, :, cols] = value.reshape(layers, rows, tile)
-
-        hidden_copy(g).start()
+            hid[core, span, :, cols] = value.reshape(blocks, rows, tile)
+
+        for each in range(g, g + many):
+            hidden_copy(each).start()
 
     def hidden_copy(g):
         span = pl.ds(g * layers, layers)
@@ -351,7 +352,7 @@
             right = hid[1, span].reshape(tall, half)
             out = jnp.dot(left, down_v[0, :, cols], preferred_element_type=jnp.float32)
             out += jnp.dot(right, down_v[1, :, cols], preferred_element_type=jnp.float32)
-            out *= weight[span].reshape(tall, weight.shape[2])[:, 0:1]
+            out *= row_weights(span, tall)
             part[span, :, cols] = out.astype(jnp.bfloat16).reshape(layers, rows, tile)
 
     def back(dz, da, db):
@@ -387,17 +388,17 @@
     up_project(0)
     straight(sequence[-1])
     edge = [g for g in range(1, groups) if g // side == 0 or g % side == 0]
-    for g in edge[:-1]:
-        up_project(g)
-    for k in range(layers // 2):
-        last(sequence[k])
-    up_project(edge[-1])
-    for k in range(layers // 2, layers):
+    inner = [g for g in range(1, groups) if g not in edge]
+    if edge == list(range(edge[0], edge[-1] + 1)):
+        up_project(edge[0], len(edge))
+    else:
+        for g in edge:
+            up_project(g)
+    for k in range(layers):
         last(sequence[k])
     for db in range(1, side):
         down_project(db * stride_b)
         send_back(0, db)
-    inner = [g for g in range(1, groups) if g not in edge]
     for g in inner:
         up_project(g)
     for da in range(1, side):

time: 94.8 us -> 95.1 us (level)
  no operation moved by 1% of the time
where the time goes in v5:
time: 95.1 us; the launch traced here: 94.9 us
  Pallas kernels  94.2 us (99%)
    pallas_call x1, Pallas kernels, gathered(): pl.pallas_call(functools.partial(exchange, side, layers), out_shape=(jax....  91.7 us
    pallas_call x1, Pallas kernels, gathered(): pl.pallas_call(settle, out_shape=(jax.ShapeDtypeStruct(mixed.shape, bf16)...  2.56 us

profile of v5, /device:TPU:8, one launch (start us, length us, event | category | flops | bytes accessed | tf_op | source)
XLA Modules:
  0.0 94.9 jit_solution(12921006216299812807)
XLA Ops:
  0.6 91.7 %shard_map.77 = (bf16[64,1792]{1,0:T(8,128)(2,1)}, f32[512,1024]{1,0:T(8,128)}) custom-call(bf16[64,1792]{1,0:T(8,128)(2,1)} %tokens_hbm.1, s32[8,64]{1,0:T(8,128)} %bitcast.10, f32[8,64]{1,0:T(8,128)} %bitcast.11, bf16[2,1792,512]{2,1,0:T(8,128)(2,1)} %bitcast.6, bf16[2,1792,512]{2,1,0:T(8,128)(2,1)} %bitcast.7, bf16[2,512,1792]{2,1,0:T(8,128)(2,1)} %bitcast.8), custom_call_target="tpu_custom_call" | custom-call | flops 12348030976 | bytes 11010048 | tf_op jit(solution)/shard_map/pallas_call | solution.py:493
  92.3 2.6 %shard_map.78 = (bf16[64,1792]{1,0:T(8,128)(2,1)}, f32[512,1024]{1,0:T(8,128)}) custom-call(bf16[64,1792]{1,0:T(8,128)(2,1)} %get-tuple-element.6.mixed_in, f32[512,1024]{1,0:T(8,128)} %get-tuple-element.7.hess_in), custom_call_target="tpu_custom_call" | custom-call | tf_op jit(solution)/shard_map/pallas_call | solution.py:543

commit v6 on v5

--- a/solution.py
+++ b/solution.py
@@ -9,6 +9,7 @@
 from jax.sharding import PartitionSpec as P
 
 MESH = pl.DeviceIdType.MESH
+PIECES = 2
 
 
 def dispatch(tokens, routes, mixing, gate_weight, up_weight, down_weight):
@@ -137,7 +138,12 @@
             device_id_type=MESH,
         )
 
-    def forward(dz, da, db):
+    piece = rows // PIECES
+
+    def cut(h):
+        return pl.ds(h * piece, piece)
+
+    def forward(dz, da, db, h):
         if db:
             source, to = slot(dz, da, 0), peer_b(db)
         elif da:
@@ -146,16 +152,21 @@
             source, to = slot(0, 0, 0), peer_z(dz)
         name = label(dz, da, db)
         here = slot(dz, da, db)
-        return (
-            remote(table.at[source], table.at[here], tab_send.at[name], tab_recv.at[name], to),
+        copies = [
             remote(
-                tok.at[core, source],
-                tok.at[core, here],
-                tok_send.at[name],
-                tok_recv.at[name],
+                tok.at[core, source, cut(h)],
+                tok.at[core, here, cut(h)],
+                tok_send.at[name, h],
+                tok_recv.at[name, h],
                 to,
-            ),
-        )
+            )
+        ]
+        if h == 0:
+            copies.insert(
+                0,
+                remote(table.at[source], table.at[here], tab_send.at[name], tab_recv.at[name], to),
+            )
+        return copies
 
     def start(copies):
         for copy in copies:
@@ -165,22 +176,22 @@
         for copy in copies:
             copy.wait_recv()
 
-    def across(where):
+    def across(where, h):
         return remote(
-            tok.at[core, where],
-            tok.at[core, where],
-            pair_send.at[where],
-            pair_recv.at[where],
+            tok.at[core, where, cut(h)],
+            tok.at[core, where, cut(h)],
+            pair_send.at[where, h],
+            pair_recv.at[where, h],
             me,
             1 - core,
         )
 
-    def from_pair(where):
+    def from_pair(where, h):
         return remote(
-            tok.at[1 - core, where],
-            tok.at[1 - core, where],
-            pair_send.at[where],
-            pair_recv.at[where],
+            tok.at[1 - core, where, cut(h)],
+            tok.at[1 - core, where, cut(h)],
+            pair_send.at[where, h],
+            pair_recv.at[where, h],
             me,
             1 - core,
         )
@@ -215,71 +226,80 @@
     def coming(k):
         return sum(jnp.where(z == place, orders[place][k], 0) for place in range(layers))
 
-    def chain(s, way, here):
+    def chain(s, way, here, h):
         source = slot(s, 0, 0)
         there = slot(here, 0, 0)
         to = me + (groups if way == 0 else -groups)
-        return (
+        copies = [
             remote(
-                table.at[source],
-                table.at[there],
-                chain_send.at[2 + way, s],
-                tab_recv.at[here],
+                tok.at[core, source, cut(h)],
+                tok.at[core, there, cut(h)],
+                chain_send.at[way, s, h],
+                tok_recv.at[here, h],
                 to,
-            ),
-            remote(
-                tok.at[core, source],
-                tok.at[core, there],
-                chain_send.at[way, s],
-                tok_recv.at[here],
-                to,
-            ),
-        )
-
-    def along(s, act):
+            )
+        ]
+        if h == 0:
+            copies.insert(
+                0,
+                remote(
+                    table.at[source],
+                    table.at[there],
+                    chain_send.at[2 + way, s, 0],
+                    tab_recv.at[here],
+                    to,
+                ),
+            )
+        return copies
+
+    def along(s, h, act):
         @pl.when((z < layers - 1) & (s <= z))
         def _():
-            for copy in chain(s, 0, s + 1):
+            for copy in chain(s, 0, s + 1, h):
                 act(copy)
 
         @pl.when((z > 0) & ((s == 0) | (s > z)))
         def _():
-            for copy in chain(s, 1, (s + layers - 1) % layers):
+            for copy in chain(s, 1, (s + layers - 1) % layers, h):
                 act(copy)
 
-    def spread(dz):
-        along(dz, lambda copy: copy.start())
+    def spread(dz, h):
+        along(dz, h, lambda copy: copy.start())
         for d in range(1, side):
-            start(forward(dz, d, 0))
-            start(forward(dz, 0, d))
-        across(slot(dz, 0, 0)).start()
-
-    def turn(dz):
+            start(forward(dz, d, 0, h))
+            start(forward(dz, 0, d, h))
+        across(slot(dz, 0, 0), h).start()
+
+    def turn(dz, h):
         for da in range(1, side):
-            arrive(forward(dz, da, 0))
+            arrive(forward(dz, da, 0, h))
             for db in range(1, side):
-                start(forward(dz, da, db))
-            across(slot(dz, da, 0)).start()
-
-    def straight(dz):
+                start(forward(dz, da, db, h))
+            across(slot(dz, da, 0), h).start()
+
+    def straight(dz, h):
         for db in range(1, side):
-            arrive(forward(dz, 0, db))
-            across(slot(dz, 0, db)).start()
-
-    def last(dz):
+            arrive(forward(dz, 0, db, h))
+            across(slot(dz, 0, db), h).start()
+
+    def last(dz, h):
         for da in range(1, side):
             for db in range(1, side):
-                arrive(forward(dz, da, db))
-                across(slot(dz, da, db)).start()
+                arrive(forward(dz, da, db, h))
+                across(slot(dz, da, db), h).start()
 
     sequence = [0] + [coming(k) for k in range(layers - 1)]
-    spread(sequence[0])
+    for h in range(PIECES):
+        spread(sequence[0], h)
     for k in range(1, layers):
-        arrive(forward(sequence[k], 0, 0))
-        spread(sequence[k])
-        turn(sequence[k - 1])
-        straight(sequence[k - 1])
-    turn(sequence[-1])
+        for h in range(PIECES):
+            arrive(forward(sequence[k], 0, 0, h))
+            spread(sequence[k], h)
+            turn(sequence[k - 1], h)
+        for h in range(PIECES):
+            straight(sequence[k - 1], h)
+    for h in range(PIECES):
+        turn(sequence[-1], h)
 
     tall = layers * rows
     tile = min(256, half)
@@ -297,7 +317,8 @@
         tall = blocks * rows
         span = pl.ds(first, blocks)
         for i in range(blocks):
-            from_pair(first + i).wait_recv()
+            for h in range(PIECES):
+                from_pair(first + i, h).wait_recv()
             mine = table[first + i, pl.ds(me, 1), 0:rows]
             column = jnp.sum(jnp.where(diagonal, mine, 0.0), axis=1, keepdims=True)
             weight[first + i] = jnp.broadcast_to(column, weight.shape[1:])
@@ -355,38 +376,40 @@
             out *= row_weights(span, tall)
             part[span, :, cols] = out.astype(jnp.bfloat16).reshape(layers, rows, tile)
 
-    def back(dz, da, db):
+    def back(dz, da, db, h):
         name = label(dz, da, db)
-        source = part.at[slot(dz, da, db)]
+        source = part.at[slot(dz, da, db), cut(h)]
         if db:
-            target, to = in_b.at[db - 1, da * layers + dz], peer_b(side - db)
+            target, to = in_b.at[db - 1, da * layers + dz, cut(h)], peer_b(side - db)
         elif da:
-            target, to = in_a.at[da - 1, dz], peer_a(side - da)
+            target, to = in_a.at[da - 1, dz, cut(h)], peer_a(side - da)
         else:
-            target, to = in_z.at[dz - 1], peer_z(layers - dz)
-        return remote(source, target, back_send.at[name], back_recv.at[name], to)
-
-    def summed(dz, da):
-        total = part[slot(dz, da, 0)].astype(jnp.float32)
+            target, to = in_z.at[dz - 1, cut(h)], peer_z(layers - dz)
+        return remote(source, target, back_send.at[name, h], back_recv.at[name, h], to)
+
+    def summed(dz, da, h):
+        total = part[slot(dz, da, 0), cut(h)].astype(jnp.float32)
         for db in range(1, side):
-            back(dz, da, db).wait_recv()
-            total += in_b[db - 1, da * layers + dz].astype(jnp.float32)
+            back(dz, da, db, h).wait_recv()
+            total += in_b[db - 1, da * layers + dz, cut(h)].astype(jnp.float32)
         if da == 0:
             for d in range(1, side):
-                back(dz, d, 0).wait_recv()
-                total += in_a[d - 1, dz].astype(jnp.float32)
+                back(dz, d, 0, h).wait_recv()
+                total += in_a[d - 1, dz, cut(h)].astype(jnp.float32)
         return total
 
     far = sorted(range(1, layers), key=lambda d: -min(d, layers - d))
 
     def send_back(da, db):
         for dz in far + [0]:
-            back(dz, da, db).start()
+            for h in range(PIECES):
+                back(dz, da, db, h).start()
 
     for load in loads[1:]:
         load.wait()
     up_project(0)
-    straight(sequence[-1])
+    for h in range(PIECES):
+        straight(sequence[-1], h)
     edge = [g for g in range(1, groups) if g // side == 0 or g % side == 0]
     inner = [g for g in range(1, groups) if g not in edge]
     if edge == list(range(edge[0], edge[-1] + 1)):
@@ -395,7 +418,8 @@
         for g in edge:
             up_project(g)
     for k in range(layers):
-        last(sequence[k])
+        for h in range(PIECES):
+            last(sequence[k], h)
     for db in range(1, side):
         down_project(db * stride_b)
         send_back(0, db)
@@ -431,32 +455,36 @@
     hessian_half(0)
     for da in range(1, side):
         for dz in far + [0]:
-            part[slot(dz, da, 0)] = summed(dz, da).astype(jnp.bfloat16)
-            back(dz, da, 0).start()
+            for h in range(PIECES):
+                part[slot(dz, da, 0), cut(h)] = summed(dz, da, h).astype(jnp.bfloat16)
+                back(dz, da, 0, h).start()
     hessian_half(1)
     store = pltpu.make_async_copy(hess_v, hess_hbm, local_sem.at[0])
     store.start()
     for dz in far:
-        part[dz] = summed(dz, 0).astype(jnp.bfloat16)
-        back(dz, 0, 0).start()
-    total = summed(0, 0)
-    for dz in range(1, layers):
-        back(dz, 0, 0).wait_recv()
-        total += in_z[dz - 1].astype(jnp.float32)
-    mixed_ref[...] = total.astype(jnp.bfloat16)
+        for h in range(PIECES):
+            part[dz, cut(h)] = summed(dz, 0, h).astype(jnp.bfloat16)
+            back(dz, 0, 0, h).start()
+    for h in range(PIECES):
+        total = summed(0, 0, h)
+        for dz in far:
+            back(dz, 0, 0, h).wait_recv()
+            total += in_z[dz - 1, cut(h)].astype(jnp.float32)
+        mixed_ref[cut(h)] = total.astype(jnp.bfloat16)
 
     store.wait()
-    for da in range(side):
-        for db in range(side):
-            for dz in range(layers):
-                across(slot(dz, da, db)).wait_send()
-                if da or db:
-                    for copy in forward(dz, da, db):
-                        copy.wait_send()
-                if dz or da or db:
-                    back(dz, da, db).wait_send()
-    for dz in range(layers):
-        along(dz, lambda copy: copy.wait_send())
+    for h in range(PIECES):
+        for da in range(side):
+            for db in range(side):
+                for dz in range(layers):
+                    across(slot(dz, da, db), h).wait_send()
+                    if da or db:
+                        for copy in forward(dz, da, db, h):
+                            copy.wait_send()
+                    if dz or da or db:
+                        back(dz, da, db, h).wait_send()
+        for dz in range(layers):
+            along(dz, h, lambda copy: copy.wait_send())
     for g in range(groups):
         hidden_copy(g).wait_send()
 
@@ -512,17 +540,17 @@
             pltpu.VMEM((layers - 1, rows, width), bf16),
             pltpu.VMEM((half, 2 * half), f32),
             dma((4,)),
+            dma((count, PIECES)),
+            dma((count, PIECES)),
             dma((count,)),
             dma((count,)),
-            dma((count,)),
-            dma((count,)),
-            dma((count,)),
-            dma((count,)),
+            dma((count, PIECES)),
+            dma((count, PIECES)),
             dma((side * side,)),
             dma((side * side,)),
-            dma((count,)),
-            dma((count,)),
-            dma((4, layers)),
+            dma((count, PIECES)),
+            dma((count, PIECES)),
+            dma((4, layers, PIECES)),
         ],
         compiler_params=pltpu.CompilerParams(
             collective_id=0, has_side_effects=True, vmem_limit_bytes=60 * 2**20

time: 95.1 us -> 97.4 us (1.024)
  Pallas kernels: 94.2 us -> 96.6 us
    pallas_call x1, Pallas kernels: 91.7 us -> 94 us  [gathered(): pl.pallas_call(functools.partial(exchange, side, layers), out_shape=(jax....]
where the time goes in v6:
time: 97.4 us; the launch traced here: 97.2 us
  Pallas kernels  96.6 us (99%)
    pallas_call x1, Pallas kernels, gathered(): pl.pallas_call(functools.partial(exchange, side, layers), out_shape=(jax....  94 us
    pallas_call x1, Pallas kernels, gathered(): pl.pallas_call(settle, out_shape=(jax.ShapeDtypeStruct(mixed.shape, bf16)...  2.56 us

profile of v6, /device:TPU:8, one launch (start us, length us, event | category | flops | bytes accessed | tf_op | source)
XLA Modules:
  0.0 97.2 jit_solution(5745555340886805936)
XLA Ops:
  0.6 94.0 %shard_map.77 = (bf16[64,1792]{1,0:T(8,128)(2,1)}, f32[512,1024]{1,0:T(8,128)}) custom-call(bf16[64,1792]{1,0:T(8,128)(2,1)} %tokens_hbm.1, s32[8,64]{1,0:T(8,128)} %bitcast.10, f32[8,64]{1,0:T(8,128)} %bitcast.11, bf16[2,1792,512]{2,1,0:T(8,128)(2,1)} %bitcast.6, bf16[2,1792,512]{2,1,0:T(8,128)(2,1)} %bitcast.7, bf16[2,512,1792]{2,1,0:T(8,128)(2,1)} %bitcast.8), custom_call_target="tpu_custom_call" | custom-call | flops 12348030976 | bytes 11010048 | tf_op jit(solution)/shard_map/pallas_call | solution.py:521
  94.6 2.6 %shard_map.78 = (bf16[64,1792]{1,0:T(8,128)(2,1)}, f32[512,1024]{1,0:T(8,128)}) custom-call(bf16[64,1792]{1,0:T(8,128)(2,1)} %get-tuple-element.6.mixed_in, f32[512,1024]{1,0:T(8,128)} %get-tuple-element.7.hess_in), custom_call_target="tpu_custom_call" | custom-call | tf_op jit(solution)/shard_map/pallas_call | solution.py:571

commit v7 on v5

--- a/solution.py
+++ b/solution.py
@@ -291,7 +291,7 @@
         wide = weight[span].reshape(count, weight.shape[2])
         return jnp.concatenate([wide] * (tile // weight.shape[2]), axis=1)
 
-    def up_project(g, many=1):
+    def up_project(g, many=1, between=None):
         first = g * layers
         blocks = many * layers
         tall = blocks * rows
@@ -302,9 +302,8 @@
             column = jnp.sum(jnp.where(diagonal, mine, 0.0), axis=1, keepdims=True)
             weight[first + i] = jnp.broadcast_to(column, weight.shape[1:])
 
-        @pl.loop(0, half // tile)
-        def _(j):
-            cols = pl.ds(pl.multiple_of(j * tile, tile), tile)
+        for j in range(half // tile):
+            cols = pl.ds(j * tile, tile)
             left = tok[0, span].reshape(tall, width)
             right = tok[1, span].reshape(tall, width)
             gate = jnp.dot(left, gate_v[0, :, cols], preferred_element_type=jnp.float32)
@@ -315,6 +314,8 @@
             value = gate / (1.0 + jnp.exp(-gate)) * upper
             value = jnp.where(chosen, value, 0.0).astype(jnp.bfloat16)
             hid[core, span, :, cols] = value.reshape(blocks, rows, tile)
+            if between is not None:
+                between(j)
 
         for each in range(g, g + many):
             hidden_copy(each).start()
@@ -389,13 +390,20 @@
     straight(sequence[-1])
     edge = [g for g in range(1, groups) if g // side == 0 or g % side == 0]
     inner = [g for g in range(1, groups) if g not in edge]
-    if edge == list(range(edge[0], edge[-1] + 1)):
-        up_project(edge[0], len(edge))
+    down_project(0)
+    share = layers // (half // tile)
+
+    def pass_on(j):
+        for k in range(j * share, j * share + share):
+            last(sequence[k])
+
+    if edge == list(range(edge[0], edge[-1] + 1)) and share * (half // tile) == layers:
+        up_project(edge[0], len(edge), pass_on)
     else:
         for g in edge:
             up_project(g)
-    for k in range(layers):
-        last(sequence[k])
+        for k in range(layers):
+            last(sequence[k])
     for db in range(1, side):
         down_project(db * stride_b)
         send_back(0, db)
@@ -407,7 +415,6 @@
         for db in range(1, side):
             down_project(da * stride_a + db * stride_b)
             send_back(da, db)
-    down_project(0)
 
     named_rows = jnp.zeros((rows, weight.shape[2]), jnp.float32)
     for s in range(weight.shape[0]):
@@ -416,24 +423,25 @@
     scale = 2.0 / count
     every = weight.shape[0] * rows
 
-    def hessian_half(h):
-        @pl.loop(0, half // tile)
-        def _(j):
-            cols = pl.ds(pl.multiple_of(j * tile, tile), tile)
-            gram = lax.dot_general(
-                hid[core, :, :, cols].reshape(every, tile),
-                hid[h].reshape(every, half),
-                (((0,), (0,)), ((), ())),
-                preferred_element_type=jnp.float32,
-            )
-            hess_v[cols, pl.ds(h * half, half)] = gram * scale
-
-    hessian_half(0)
+    def hessian_tile(h, j):
+        cols = pl.ds(j * tile, tile)
+        gram = lax.dot_general(
+            hid[core, :, :, cols].reshape(every, tile),
+            hid[h].reshape(every, half),
+            (((0,), (0,)), ((), ())),
+            preferred_element_type=jnp.float32,
+        )
+        hess_v[cols, pl.ds(h * half, half)] = gram * scale
+
+    tiles = [(h, j) for h in range(2) for j in range(half // tile)]
     for da in range(1, side):
         for dz in far + [0]:
             part[slot(dz, da, 0)] = summed(dz, da).astype(jnp.bfloat16)
             back(dz, da, 0).start()
-    hessian_half(1)
+            if tiles:
+                hessian_tile(*tiles.pop(0))
+    for rest in tiles:
+        hessian_tile(*rest)
     store = pltpu.make_async_copy(hess_v, hess_hbm, local_sem.at[0])
     store.start()
     for dz in far:

time: 95.1 us -> 98 us (1.030)
  Pallas kernels: 94.2 us -> 97 us
    pallas_call x1, Pallas kernels: 91.7 us -> 94.4 us  [gathered(): pl.pallas_call(functools.partial(exchange, side, layers), out_shape=(jax....]
where the time goes in v7:
time: 98 us; the launch traced here: 97.6 us
  Pallas kernels  97 us (99%)
    pallas_call x1, Pallas kernels, gathered(): pl.pallas_call(functools.partial(exchange, side, layers), out_shape=(jax....  94.4 us
    pallas_call x1, Pallas kernels, gathered(): pl.pallas_call(settle, out_shape=(jax.ShapeDtypeStruct(mixed.shape, bf16)...  2.56 us

profile of v7, /device:TPU:8, one launch (start us, length us, event | category | flops | bytes accessed | tf_op | source)
XLA Modules:
  0.0 97.6 jit_solution(18352425064311395536)
XLA Ops:
  0.6 94.4 %shard_map.77 = (bf16[64,1792]{1,0:T(8,128)(2,1)}, f32[512,1024]{1,0:T(8,128)}) custom-call(bf16[64,1792]{1,0:T(8,128)(2,1)} %tokens_hbm.1, s32[8,64]{1,0:T(8,128)} %bitcast.10, f32[8,64]{1,0:T(8,128)} %bitcast.11, bf16[2,1792,512]{2,1,0:T(8,128)(2,1)} %bitcast.6, bf16[2,1792,512]{2,1,0:T(8,128)(2,1)} %bitcast.7, bf16[2,512,1792]{2,1,0:T(8,128)(2,1)} %bitcast.8), custom_call_target="tpu_custom_call" | custom-call | flops 12348030976 | bytes 11010048 | tf_op jit(solution)/shard_map/pallas_call | solution.py:501
  95.0 2.6 %shard_map.78 = (bf16[64,1792]{1,0:T(8,128)(2,1)}, f32[512,1024]{1,0:T(8,128)}) custom-call(bf16[64,1792]{1,0:T(8,128)(2,1)} %get-tuple-element.6.mixed_in, f32[512,1024]{1,0:T(8,128)} %get-tuple-element.7.hess_in), custom_call_target="tpu_custom_call" | custom-call | tf_op jit(solution)/shard_map/pallas_call | solution.py:551

commit v8 on v4

--- a/solution.py
+++ b/solution.py
@@ -257,12 +257,9 @@
     def turn(dz):
         for da in range(1, side):
             arrive(forward(dz, da, 0))
-            across(slot(dz, da, 0)).start()
-
-    def finish(dz):
-        for da in range(1, side):
             for db in range(1, side):
                 start(forward(dz, da, db))
+            across(slot(dz, da, 0)).start()
 
     def straight(dz):
         for db in range(1, side):
@@ -282,10 +279,7 @@
         spread(sequence[k])
         turn(sequence[k - 1])
         straight(sequence[k - 1])
-    for k in range(layers - 1):
-        finish(sequence[k])
     turn(sequence[-1])
-    finish(sequence[-1])
 
     tall = layers * rows
     tile = min(256, half)
@@ -376,10 +370,8 @@
                 total += in_a[d - 1, dz].astype(jnp.float32)
         return total
 
-    far = sorted(range(1, layers), key=lambda d: -min(d, layers - d))
-
     def send_back(da, db):
-        for dz in far + [0]:
+        for dz in range(layers):
             back(dz, da, db).start()
 
     for load in loads[1:]:
@@ -414,8 +406,8 @@
     count = jnp.sum(named_rows, axis=0, keepdims=True)[:, 0:1]
     scale = 2.0 / count
     every = weight.shape[0] * rows
-
-    def hessian_half(h):
+    for h in range(2):
+
         @pl.loop(0, half // tile)
         def _(j):
             cols = pl.ds(pl.multiple_of(j * tile, tile), tile)
@@ -427,14 +419,14 @@
             )
             hess_v[cols, pl.ds(h * half, half)] = gram * scale
 
-    hessian_half(0)
+    store = pltpu.make_async_copy(hess_v, hess_hbm, local_sem.at[0])
+    store.start()
+
+    far = sorted(range(1, layers), key=lambda d: -min(d, layers - d))
     for da in range(1, side):
         for dz in far + [0]:
             part[slot(dz, da, 0)] = summed(dz, da).astype(jnp.bfloat16)
             back(dz, da, 0).start()
-    hessian_half(1)
-    store = pltpu.make_async_copy(hess_v, hess_hbm, local_sem.at[0])
-    store.start()
     for dz in far:
         part[dz] = summed(dz, 0).astype(jnp.bfloat16)
         back(dz, 0, 0).start()

time: 94.8 us -> 92 us (0.970)
  Pallas kernels: 93.4 us -> 90.6 us
    pallas_call x1, Pallas kernels: 90.8 us -> 88 us  [gathered(): pl.pallas_call(functools.partial(exchange, side, layers), out_shape=(jax....]
where the time goes in v8:
time: 92 us; the launch traced here: 91.2 us
  Pallas kernels  90.6 us (98%)
    pallas_call x1, Pallas kernels, gathered(): pl.pallas_call(functools.partial(exchange, side, layers), out_shape=(jax....  88 us
    pallas_call x1, Pallas kernels, gathered(): pl.pallas_call(settle, out_shape=(jax.ShapeDtypeStruct(mixed.shape, bf16)...  2.56 us

profile of v8, /device:TPU:8, one launch (start us, length us, event | category | flops | bytes accessed | tf_op | source)
XLA Modules:
  0.0 91.2 jit_solution(14581639954858631148)
XLA Ops:
  0.6 88.0 %shard_map.77 = (bf16[64,1792]{1,0:T(8,128)(2,1)}, f32[512,1024]{1,0:T(8,128)}) custom-call(bf16[64,1792]{1,0:T(8,128)(2,1)} %tokens_hbm.1, s32[8,64]{1,0:T(8,128)} %bitcast.10, f32[8,64]{1,0:T(8,128)} %bitcast.11, bf16[2,1792,512]{2,1,0:T(8,128)(2,1)} %bitcast.6, bf16[2,1792,512]{2,1,0:T(8,128)(2,1)} %bitcast.7, bf16[2,512,1792]{2,1,0:T(8,128)(2,1)} %bitcast.8), custom_call_target="tpu_custom_call" | custom-call | flops 12348030976 | bytes 11010048 | tf_op jit(solution)/shard_map/pallas_call | solution.py:484
  88.7 2.6 %shard_map.78 = (bf16[64,1792]{1,0:T(8,128)(2,1)}, f32[512,1024]{1,0:T(8,128)}) custom-call(bf16[64,1792]{1,0:T(8,128)(2,1)} %get-tuple-element.6.mixed_in, f32[512,1024]{1,0:T(8,128)} %get-tuple-element.7.hess_in), custom_call_target="tpu_custom_call" | custom-call | tf_op jit(solution)/shard_map/pallas_call | solution.py:534

commit v9 on v8

--- a/solution.py
+++ b/solution.py
@@ -371,7 +371,7 @@
         return total
 
     def send_back(da, db):
-        for dz in range(layers):
+        for dz in [*range(2, layers), 1, 0]:
             back(dz, da, db).start()
 
     for load in loads[1:]:

time: 92 us -> 91.6 us (level)
  the two profiles are of different devices: /device:TPU:8 before, /device:TPU:9 now
where the time goes in v9:
time: 91.6 us; the launch traced here: 91.4 us
  Pallas kernels  90.8 us (99%)
    pallas_call x1, Pallas kernels, gathered(): pl.pallas_call(functools.partial(exchange, side, layers), out_shape=(jax....  88.2 us
    pallas_call x1, Pallas kernels, gathered(): pl.pallas_call(settle, out_shape=(jax.ShapeDtypeStruct(mixed.shape, bf16)...  2.56 us

profile of v9, /device:TPU:9, one launch (start us, length us, event | category | flops | bytes accessed | tf_op | source)
XLA Modules:
  0.0 91.4 jit_solution(6497523623858995978)
XLA Ops:
  0.6 88.2 %shard_map.77 = (bf16[64,1792]{1,0:T(8,128)(2,1)}, f32[512,1024]{1,0:T(8,128)}) custom-call(bf16[64,1792]{1,0:T(8,128)(2,1)} %tokens_hbm.1, s32[8,64]{1,0:T(8,128)} %bitcast.10, f32[8,64]{1,0:T(8,128)} %bitcast.11, bf16[2,1792,512]{2,1,0:T(8,128)(2,1)} %bitcast.6, bf16[2,1792,512]{2,1,0:T(8,128)(2,1)} %bitcast.7, bf16[2,512,1792]{2,1,0:T(8,128)(2,1)} %bitcast.8), custom_call_target="tpu_custom_call" | custom-call | flops 12348030976 | bytes 11010048 | tf_op jit(solution)/shard_map/pallas_call | solution.py:484
  88.9 2.6 %shard_map.78 = (bf16[64,1792]{1,0:T(8,128)(2,1)}, f32[512,1024]{1,0:T(8,128)}) custom-call(bf16[64,1792]{1,0:T(8,128)(2,1)} %get-tuple-element.6.mixed_in, f32[512,1024]{1,0:T(8,128)} %get-tuple-element.7.hess_in), custom_call_target="tpu_custom_call" | custom-call | tf_op jit(solution)/shard_map/pallas_call | solution.py:534
